TPU v7x, 32 devices: a whole 2x2x4 slice. The times are simulated.
32 devices in a mesh: dp: 2 (over core), expert: 16 (over z, y, x).
Axes of the slice: x: 2, y: 2, z: 4, core: 2. Of those that a mesh axis runs over, the one named last changes fastest.
Arguments:
- tokens: bfloat16 [2, 2048, 1536], P(None, ('dp', 'expert')), may hold values from -6 to 6
- cotangent: bfloat16 [2, 2048, 1536], P(None, ('dp', 'expert')), may hold values from -6 to 6
- segments: int32 [2, 2048], P(None, ('dp', 'expert')), may hold values from 0 to 4, as said below
- positions: int32 [2, 2048], P(None, ('dp', 'expert')), may hold values from 0 to 2046, as said below
- routes: int32 [2, 2048, 8], P(None, ('dp', 'expert')), may hold values from 0 to 15, all different within a row; in each aligned block of 64 rows (0 to 63, 64 to 127, ..., all dimensions but the last counted through in order) at most 64 rows name the same one
- w_qkv: bfloat16 [1536, 2560], P(('dp', 'expert')), may hold values from -0.15625 to 0.15625
- w_out: bfloat16 [1536, 1536], P(('dp', 'expert')), may hold values from -1.25 to 1.25
- w_router: bfloat16 [1536, 16], P(('dp', 'expert')), may hold values from -0.078125 to 0.078125
- norm_attn: bfloat16 [1536], P(('dp', 'expert')), may hold values from 0.5 to 1.5
- norm_ffn: bfloat16 [1536], P(('dp', 'expert')), may hold values from 0.5 to 1.5
- w_gate_up: bfloat16 [16, 1536, 1024], P('expert', 'dp'), may hold values from -0.15625 to 0.15625
- w_down: bfloat16 [16, 512, 1536], P('expert', 'dp'), may hold values from -0.75 to 0.75
Outputs:
- mixed: bfloat16 [2, 2048, 1536], P(None, ('dp', 'expert'))
- grad_tokens: float32 [2, 2048, 1536], P(None, ('dp', 'expert'))
- grad_qkv: float32 [1536, 2560], P(('dp', 'expert'))
- grad_out: float32 [1536, 1536], P(('dp', 'expert'))
- grad_router: float32 [1536, 16], P(('dp', 'expert'))
- grad_norm_attn: float32 [1536], P(('dp', 'expert'))
- grad_norm_ffn: float32 [1536], P(('dp', 'expert'))
- grad_gate_up: float32 [16, 1536, 1024], P('expert', 'dp')
- grad_down: float32 [16, 512, 1536], P('expert', 'dp')
Inputs may be any that keep to these rules, and one draw needn't show every extreme that they name: `segments`: within each sequence of 1024 tokens (one micro-batch, one index of dp) the numbers never fall. `positions`: within a document they rise by one from token to token. `routes`: each row names 8 different experts; among the 64 rows of one device in one micro-batch no expert is named more than 64 times.
All inputs are finite; a program needn't handle non-finite values.
Results may differ from a plain program's by a relative error of at most 0.02.
Values may be sent and summed in bfloat16 or wider, within the bound.
No kernel may reach another device: no remote copies, remote signals or barrier semaphores. Data moves between devices by JAX's collectives and lax.ppermute only.
A program may use at most 192 MiB of HBM per device.

v0:
```python
import jax
import jax.numpy as jnp
from jax import lax
from jax.sharding import PartitionSpec as P

HEADS = 24
KV_HEADS = 8
HEAD_DIM = 64
EXP_FF = 512
TOP = 8


epsilon = 1e-06
rope_base = 10000.0
masked = -1e30


def for_sending(shard):

    def short(part):
        return part.astype(jnp.bfloat16) if part.dtype == jnp.float32 else part

    return jax.tree.map(short, shard)


def silu_value(inputs):
    return inputs / (1.0 + jnp.exp(-inputs))


def rotate(vectors, places, direction):
    half_dim = vectors.shape[-1] // 2
    frequency = rope_base ** (-jnp.arange(half_dim, dtype=jnp.float32) / half_dim)
    angles = places.astype(jnp.float32)[:, None] * frequency[None, :]
    cosine = jnp.cos(angles)[:, None, :]
    sine_part = direction * jnp.sin(angles)[:, None, :]
    first_half = vectors[..., :half_dim]
    second_half = vectors[..., half_dim:]
    return jnp.concatenate(
        [
            first_half * cosine - second_half * sine_part,
            second_half * cosine + first_half * sine_part,
        ],
        -1,
    )


def normed(inputs, scales):
    return inputs * lax.rsqrt(jnp.mean(inputs * inputs, -1, keepdims=True) + epsilon) * scales


def score_block(queries, key_part, key_start, key_docs, query_places, query_docs):
    scores = (
        jnp.einsum("tgrd,ngd->grtn", queries, key_part, preferred_element_type=jnp.float32) * 0.125
    )
    key_places = key_start + jnp.arange(key_part.shape[0], dtype=jnp.int32)
    allowed = (query_docs[:, None] == key_docs[None, :]) & (
        key_places[None, :] <= query_places[:, None]
    )
    return (jnp.where(allowed[None, None], scores, masked), allowed)


def gather_dense(w_qkv, w_out, w_router, norm_attn, norm_ffn):
    gathered = (
        lax.all_gather(w_qkv, ("dp", "expert"), axis=0, tiled=True),
        lax.all_gather(w_out, ("dp", "expert"), axis=0, tiled=True),
        lax.all_gather(w_router, ("dp", "expert"), axis=0, tiled=True),
        lax.all_gather(norm_attn, ("dp", "expert"), axis=0, tiled=True),
        lax.all_gather(norm_ffn, ("dp", "expert"), axis=0, tiled=True),
    )
    return (
        gathered[0],
        gathered[1],
        gathered[2],
        gathered[3].astype(jnp.float32),
        gathered[4].astype(jnp.float32),
    )


def gather_expert(w_gate_up, w_down):
    gathered = (
        lax.all_gather(w_gate_up, "dp", axis=1, tiled=True),
        lax.all_gather(w_down, "dp", axis=1, tiled=True),
    )
    return (gathered[0][0], gathered[1][0])


def reduce_dense(grad_terms):
    return lax.psum_scatter(grad_terms, ("dp", "expert"), scatter_dimension=0, tiled=True)


def reduce_expert(grad_terms):
    return jax.tree.map(
        lambda part: part.astype(jnp.float32),
        lax.psum_scatter(for_sending(grad_terms), "dp", scatter_dimension=1, tiled=True),
    )


def combine_terms(running, addend):
    if running is None:
        return addend
    return tuple((earlier + current for earlier, current in zip(running, addend)))


def on_device(
    tokens,
    cotangent,
    segments,
    positions,
    routes,
    w_qkv,
    w_out,
    w_router,
    norm_attn,
    norm_ffn,
    w_gate_up,
    w_down,
):
    batches = tokens.shape[0]
    local_rows = tokens.shape[1]
    model_width = tokens.shape[2]
    expert_count = w_router.shape[1]
    capacity = 2 * local_rows * TOP // expert_count
    query_width = HEADS * HEAD_DIM
    key_width = KV_HEADS * HEAD_DIM
    group_size = HEADS // KV_HEADS
    shard_index = lax.axis_index("expert")
    query_places = shard_index * local_rows + jnp.arange(local_rows, dtype=jnp.int32)
    sequence_docs = lax.all_gather(segments, "expert", axis=1, tiled=True)
    expert_numbers = jnp.arange(expert_count, dtype=jnp.int32)
    outputs = []
    input_grads = []
    dense_total = None
    expert_total = None
    for micro_step in range(batches):
        dense_weights = gather_dense(w_qkv, w_out, w_router, norm_attn, norm_ffn)
        expert_weights = gather_expert(w_gate_up, w_down)
        qkv_full, out_full, router_full, gain_first, gain_second = dense_weights
        gate_up_full, down_full = expert_weights
        residual = tokens[micro_step].astype(jnp.float32)
        token_places = positions[micro_step]
        token_routes = routes[micro_step]
        group_docs = sequence_docs[micro_step]
        local_docs = segments[micro_step]
        normed_first, first_pull = jax.vjp(normed, residual, gain_first)
        first_low = normed_first.astype(jnp.bfloat16)
        projected = jnp.dot(first_low, qkv_full, preferred_element_type=jnp.float32)
        query_rot = rotate(
            projected[:, :query_width].reshape(local_rows, HEADS, HEAD_DIM), token_places, 1.0
        ).astype(jnp.bfloat16)
        key_rot = rotate(
            projected[:, query_width : query_width + key_width].reshape(
                local_rows, KV_HEADS, HEAD_DIM
            ),
            token_places,
            1.0,
        ).astype(jnp.bfloat16)
        value_low = projected[:, query_width + key_width :].astype(jnp.bfloat16)
        key_value = jnp.concatenate([key_rot.reshape(local_rows, key_width), value_low], 1)
        query_group = query_rot.reshape(local_rows, KV_HEADS, group_size, HEAD_DIM)
        piece_rows = lax.all_gather(key_value, "expert", axis=0, tiled=True)
        row_start = jnp.int32(0)
        row_max = jnp.full((KV_HEADS, group_size, local_rows), masked, jnp.float32)
        row_total = jnp.zeros((KV_HEADS, group_size, local_rows), jnp.float32)
        weighted = jnp.zeros((KV_HEADS, group_size, local_rows, HEAD_DIM), jnp.float32)
        piece_count = piece_rows.shape[0]
        for offset in range(0, piece_count, 512):
            block_size = min(512, piece_count - offset)
            block_rows = piece_rows[offset : offset + block_size]
            key_part = block_rows[:, :key_width].reshape(block_size, KV_HEADS, HEAD_DIM)
            value_part = block_rows[:, key_width:].reshape(block_size, KV_HEADS, HEAD_DIM)
            key_docs = lax.dynamic_slice_in_dim(group_docs, offset, block_size, 0)
            scores, allowed = score_block(
                query_group, key_part, row_start + offset, key_docs, query_places, local_docs
            )
            new_max = jnp.maximum(row_max, jnp.max(scores, -1))
            weight = jnp.where(allowed[None, None], jnp.exp(scores - new_max[..., None]), 0.0)
            factor = jnp.exp(row_max - new_max)
            row_total = row_total * factor + jnp.sum(weight, -1)
            weighted = weighted * factor[..., None] + jnp.einsum(
                "grtn,ngd->grtd",
                weight.astype(jnp.bfloat16),
                value_part,
                preferred_element_type=jnp.float32,
            )
            row_max = new_max
        row_max, row_total, weighted = (row_max, row_total, weighted)
        attended = weighted / row_total[..., None]
        log_total = row_max + jnp.log(row_total)
        attended_low = (
            jnp.transpose(attended, (2, 0, 1, 3))
            .reshape(local_rows, query_width)
            .astype(jnp.bfloat16)
        )
        y_one = residual + jnp.einsum(
            "tq,dq->td", attended_low, out_full, preferred_element_type=jnp.float32
        )
        normed_second, second_pull = jax.vjp(normed, y_one, gain_second)
        second_low = normed_second.astype(jnp.bfloat16)
        logits = jnp.dot(second_low, router_full, preferred_element_type=jnp.float32)
        raised = jnp.exp(logits - jnp.max(logits, -1, keepdims=True))
        router_probs = raised / jnp.sum(raised, -1, keepdims=True)
        chosen = (token_routes[:, :, None] == expert_numbers[None, None, :]).astype(jnp.float32)
        picked = jnp.sum(chosen * router_probs[:, None, :], -1)
        pick_total = jnp.sum(picked, -1, keepdims=True)
        gates = picked / pick_total
        flat_routes = token_routes.reshape(-1)
        expert_hits = (flat_routes[:, None] == expert_numbers[None, :]).astype(jnp.int32)
        slot_rank = jnp.sum((jnp.cumsum(expert_hits, 0) - expert_hits) * expert_hits, 1)
        slot_index = flat_routes * capacity + slot_rank
        source_row = (
            jnp.zeros((expert_count * capacity,), jnp.int32)
            .at[slot_index]
            .set(jnp.arange(local_rows * TOP, dtype=jnp.int32))
        )
        filled = jnp.zeros((expert_count * capacity,), jnp.bool_).at[slot_index].set(True)
        outgoing = jnp.where(
            filled[:, None], second_low[source_row // TOP], jnp.zeros((), jnp.bfloat16)
        ).reshape(expert_count, capacity, model_width)
        arrived = lax.all_to_all(outgoing, "expert", split_axis=0, concat_axis=0, tiled=True)
        sources = arrived.shape[0]
        slot_count = arrived.shape[1]
        flat_rows = arrived.reshape(sources * slot_count, model_width)
        gate_up = jnp.dot(flat_rows, gate_up_full, preferred_element_type=jnp.float32)
        hidden = (silu_value(gate_up[:, :EXP_FF]) * gate_up[:, EXP_FF:]).astype(jnp.bfloat16)
        result = jnp.dot(hidden, down_full, preferred_element_type=jnp.float32).astype(jnp.bfloat16)
        returned = lax.all_to_all(
            result.reshape(sources, slot_count, model_width),
            "expert",
            split_axis=0,
            concat_axis=0,
            tiled=True,
        )
        returned, kept_gate_up, kept_hidden, kept_arrived = (
            returned,
            gate_up.reshape(sources, slot_count, 2 * EXP_FF),
            hidden.reshape(sources, slot_count, EXP_FF),
            arrived,
        )
        expert_rows_out = returned.reshape(expert_count * capacity, model_width)[
            slot_index
        ].reshape(local_rows, TOP, model_width)
        mixed = y_one + jnp.sum(gates[:, :, None] * expert_rows_out.astype(jnp.float32), 1)
        outputs.append(mixed.astype(jnp.bfloat16))
        qkv_full, out_full, router_full, gain_first, gain_second = gather_dense(
            w_qkv, w_out, w_router, norm_attn, norm_ffn
        )
        gate_up_full, down_full = gather_expert(w_gate_up, w_down)
        grad_mixed = cotangent[micro_step].astype(jnp.float32)
        grad_gates = jnp.sum(grad_mixed[:, None, :] * expert_rows_out.astype(jnp.float32), -1)
        grad_rows = (
            (gates[:, :, None] * grad_mixed[:, None, :])
            .astype(jnp.bfloat16)
            .reshape(local_rows * TOP, model_width)
        )
        grad_outgoing = jnp.where(
            filled[:, None], grad_rows[source_row], jnp.zeros((), jnp.bfloat16)
        ).reshape(expert_count, capacity, model_width)
        grad_arrived = lax.all_to_all(
            grad_outgoing, "expert", split_axis=0, concat_axis=0, tiled=True
        )
        grad_flat = grad_arrived.reshape(-1, model_width)
        gate_values = kept_gate_up.reshape(-1, 2 * EXP_FF)[:, :EXP_FF]
        up_values = kept_gate_up.reshape(-1, 2 * EXP_FF)[:, EXP_FF:]
        hidden_rows = kept_hidden.reshape(-1, EXP_FF)
        input_rows = kept_arrived.reshape(-1, model_width)
        grad_hidden = jnp.einsum(
            "nd,fd->nf", grad_flat, down_full, preferred_element_type=jnp.float32
        )
        grad_down = jnp.einsum(
            "nf,nd->fd", hidden_rows, grad_flat, preferred_element_type=jnp.float32
        )
        sigmoid = 1.0 / (1.0 + jnp.exp(-gate_values))
        grad_gate_part = grad_hidden * up_values * sigmoid * (1.0 + gate_values * (1.0 - sigmoid))
        grad_up_part = grad_hidden * gate_values * sigmoid
        grad_pair = jnp.concatenate([grad_gate_part, grad_up_part], 1).astype(jnp.bfloat16)
        grad_gate_up = jnp.einsum(
            "nd,nf->df", input_rows, grad_pair, preferred_element_type=jnp.float32
        )
        back_rows = jnp.einsum(
            "nf,df->nd", grad_pair, gate_up_full, preferred_element_type=jnp.float32
        ).astype(jnp.bfloat16)
        came_back = lax.all_to_all(
            back_rows.reshape(kept_arrived.shape), "expert", split_axis=0, concat_axis=0, tiled=True
        )
        grad_from_experts = jnp.sum(
            came_back.reshape(expert_count * capacity, model_width)[slot_index]
            .reshape(local_rows, TOP, model_width)
            .astype(jnp.float32),
            1,
        )
        grad_picked = (grad_gates - jnp.sum(grad_gates * gates, -1, keepdims=True)) / pick_total
        grad_probs = jnp.sum(chosen * grad_picked[:, :, None], 1)
        grad_logits = (
            router_probs * (grad_probs - jnp.sum(router_probs * grad_probs, -1, keepdims=True))
        ).astype(jnp.bfloat16)
        grad_router = jnp.einsum(
            "td,te->de", second_low, grad_logits, preferred_element_type=jnp.float32
        )
        grad_second = grad_from_experts + jnp.einsum(
            "te,de->td", grad_logits, router_full, preferred_element_type=jnp.float32
        )
        grad_y_norm, grad_gain_second = second_pull(grad_second)
        grad_y = grad_mixed + grad_y_norm
        grad_branch = grad_y.astype(jnp.bfloat16)
        grad_out = jnp.einsum(
            "td,tq->dq", grad_branch, attended_low, preferred_element_type=jnp.float32
        )
        grad_attended = jnp.einsum(
            "td,dq->tq", grad_branch, out_full, preferred_element_type=jnp.float32
        ).astype(jnp.bfloat16)
        grad_group = grad_attended.reshape(local_rows, KV_HEADS, group_size, HEAD_DIM)
        row_delta = jnp.sum(
            jnp.transpose(grad_group.astype(jnp.float32), (1, 2, 0, 3)) * attended, -1
        )
        every_key = lax.all_gather(key_value, "expert", axis=0, tiled=True)
        key_total = every_key.shape[0]
        key_block = min(512, key_total)

        def key_step(grad_query_acc, block_number):
            block_start = block_number * key_block
            block_rows = lax.dynamic_slice_in_dim(every_key, block_start, key_block, 0)
            key_part = block_rows[:, :key_width].reshape(key_block, KV_HEADS, HEAD_DIM)
            value_part = block_rows[:, key_width:].reshape(key_block, KV_HEADS, HEAD_DIM)
            key_docs = lax.dynamic_slice_in_dim(group_docs, block_start, key_block, 0)
            scores, allowed = score_block(
                query_group, key_part, block_start, key_docs, query_places, local_docs
            )
            weight = jnp.where(allowed[None, None], jnp.exp(scores - log_total[..., None]), 0.0)
            grad_weight = jnp.einsum(
                "tgrd,ngd->grtn", grad_group, value_part, preferred_element_type=jnp.float32
            )
            grad_scores = (weight * (grad_weight - row_delta[..., None])).astype(jnp.bfloat16)
            grad_query_acc = (
                grad_query_acc
                + jnp.einsum(
                    "grtn,ngd->tgrd", grad_scores, key_part, preferred_element_type=jnp.float32
                )
                * 0.125
            )
            grad_keys = (
                jnp.einsum(
                    "grtn,tgrd->ngd", grad_scores, query_group, preferred_element_type=jnp.float32
                )
                * 0.125
            )
            grad_values = jnp.einsum(
                "grtn,tgrd->ngd",
                weight.astype(jnp.bfloat16),
                grad_group,
                preferred_element_type=jnp.float32,
            )
            return (
                grad_query_acc,
                jnp.concatenate(
                    [
                        grad_keys.reshape(key_block, key_width),
                        grad_values.reshape(key_block, key_width),
                    ],
                    1,
                ),
            )

        grad_query_rot, grad_key_value = lax.scan(
            key_step,
            jnp.zeros((local_rows, KV_HEADS, group_size, HEAD_DIM), jnp.float32),
            jnp.arange(key_total // key_block, dtype=jnp.int32),
        )
        grad_key_value_own = lax.psum_scatter(
            grad_key_value.reshape(key_total, 2 * key_width).astype(jnp.bfloat16),
            "expert",
            scatter_dimension=0,
            tiled=True,
        ).astype(jnp.float32)
        grad_query = (
            rotate(grad_query_rot.reshape(local_rows, HEADS, HEAD_DIM), token_places, -1.0)
            .astype(jnp.bfloat16)
            .reshape(local_rows, query_width)
        )
        grad_key = (
            rotate(
                grad_key_value_own[:, :key_width].reshape(local_rows, KV_HEADS, HEAD_DIM),
                token_places,
                -1.0,
            )
            .astype(jnp.bfloat16)
            .reshape(local_rows, key_width)
        )
        grad_value = grad_key_value_own[:, key_width:].astype(jnp.bfloat16)
        grad_projected = jnp.concatenate([grad_query, grad_key, grad_value], 1)
        grad_qkv = jnp.einsum(
            "td,tc->dc", first_low, grad_projected, preferred_element_type=jnp.float32
        )
        grad_first = jnp.einsum(
            "tc,dc->td", grad_projected, qkv_full, preferred_element_type=jnp.float32
        )
        grad_x_norm, grad_gain_first = first_pull(grad_first)
        input_grads.append(grad_y + grad_x_norm)
        dense_terms = (grad_qkv, grad_out, grad_router, grad_gain_first, grad_gain_second)
        expert_terms = (grad_gate_up[None], grad_down[None])
        dense_total = combine_terms(dense_total, dense_terms)
        expert_total = combine_terms(expert_total, expert_terms)
    dense_total = reduce_dense(dense_total)
    expert_total = reduce_expert(expert_total)
    mixed_out = jnp.stack(outputs, 0)
    grad_tokens = jnp.stack(input_grads, 0)
    return (
        mixed_out,
        grad_tokens,
        dense_total[0],
        dense_total[1],
        dense_total[2],
        dense_total[3],
        dense_total[4],
        expert_total[0],
        expert_total[1],
    )


def solution(mesh):
    placed = (
        P(None, ("dp", "expert"), None),
        P(None, ("dp", "expert"), None),
        P(None, ("dp", "expert")),
        P(None, ("dp", "expert")),
        P(None, ("dp", "expert"), None),
        P(("dp", "expert"), None),
        P(("dp", "expert"), None),
        P(("dp", "expert"), None),
        P(("dp", "expert")),
        P(("dp", "expert")),
        P("expert", "dp", None),
        P("expert", "dp", None),
    )
    return jax.shard_map(
        on_device,
        mesh=mesh,
        in_specs=placed,
        out_specs=(
            P(None, ("dp", "expert"), None),
            P(None, ("dp", "expert"), None),
            P(("dp", "expert"), None),
            P(("dp", "expert"), None),
            P(("dp", "expert"), None),
            P(("dp", "expert")),
            P(("dp", "expert")),
            P("expert", "dp", None),
            P("expert", "dp", None),
        ),
        check_vma=False,
    )
```

profile of v0, /device:TPU:0, one launch (start us, length us, event | category | flops | bytes accessed | tf_op | source)
XLA Modules:
  0.0 1569.9 jit_solution(17648657859848180693)
XLA Ops:
  10.5 42.5 %all-reduce.5 = (bf16[1536]{0:T(1024)(128)(2,1)S(1)}, bf16[1536]{0:T(1024)(128)(2,1)S(1)}) all-reduce(bf16[1536]{0:T(1024)(128)(2,1)S(1)} %dynamic-update-slice, bf16[1536]{0:T(1024)(128)(2,1)S(1)} %dynamic-update-slice.1), channel_id=1, replica_groups=mesh['dp'=2,'expert'=16] {'dp','expert'}, use_global_device_ids=true, to_apply=%add | all-reduce | flops 3072 | bytes 12288
  56.6 33.8 %all-gather.9.cloned.1.call-done = bf16[1536,2560]{1,0:T(8,128)(2,1)} async-done(((bf16[48,2560]{1,0:T(8,128)(2,1)}), bf16[1536,2560]{1,0:T(8,128)(2,1)}) %all-gather.9.cloned.1.call-update) | async-done | bytes 7864336 | tf_op jit(solution)/shard_map/all_gather | solution.py:64
  98.2 38.3 %all-gather = s32[16,64,2]{1,2,0:T(2,128)S(1)} all-gather(s32[1,64,2]{1,2,0:T(2,128)S(1)} %bitcast.672), channel_id=1, replica_groups=mesh['dp'=2,'expert'=16] {'expert'}, dimensions={0}, use_global_device_ids=true | all-gather | bytes 8704 | tf_op jit(solution)/shard_map/all_gather | solution.py:128
  136.6 64.5 %all-gather.1 = bf16[32,48,16]{1,2,0:T(8,128)(2,1)S(1)} all-gather(bf16[1,48,16]{1,2,0:T(8,128)(2,1)S(1)} %bitcast.671), channel_id=1, replica_groups=mesh['dp'=2,'expert'=16] {'dp','expert'}, dimensions={0}, use_global_device_ids=true | all-gather | bytes 50688 | tf_op jit(solution)/shard_map/all_gather | solution.py:66
  246.7 74.5 %all_to_all.40 = bf16[16,64,1536]{2,1,0:T(8,128)(2,1)S(1)} all-to-all(bf16[16,64,1536]{2,1,0:T(8,128)(2,1)S(1)} %get-tuple-element.503), channel_id=1, replica_groups=mesh['dp'=2,'expert'=16] {'expert'}, dimensions={0} | all-to-all | bytes 6291456 | tf_op jit(solution)/shard_map/all_to_all | solution.py:219
  326.9 14.1 all-gather.15.cloned.1.call-done
  353.3 32.5 %all-to-all-done.4 = bf16[16,64,1536]{2,1,0:T(8,128)(2,1)} async-done(((bf16[16,64,1536]{2,1,0:T(8,128)(2,1)}), bf16[16,64,1536]{2,1,0:T(8,128)(2,1)}, u32[]{:S(2)}, u32[]{:S(2)}) %all-to-all-start.4) | async-done | bytes 3145760 | tf_op jit(solution)/shard_map/all_to_all | solution.py:258
  396.9 14.0 all-to-all-start.1
  434.7 44.3 %all-to-all-done.1 = bf16[16,64,1536]{2,1,0:T(8,128)(2,1)S(1)} async-done(((bf16[16,64,1536]{2,1,0:T(8,128)(2,1)}), bf16[16,64,1536]{2,1,0:T(8,128)(2,1)S(1)}, u32[]{:S(2)}, u32[]{:S(2)}) %all-to-all-start.1) | async-done | bytes 3145760 | tf_op jit(solution)/shard_map/all_to_all | solution.py:226
  479.0 21.6 %all-to-all-start.5 = ((bf16[16,64,1536]{2,1,0:T(8,128)(2,1)}), bf16[16,64,1536]{2,1,0:T(8,128)(2,1)}, u32[]{:S(2)}, u32[]{:S(2)}) async-start(bf16[16,64,1536]{2,1,0:T(8,128)(2,1)} %bitcast.629), calls=%async_computation.5 | async-start | bytes 6291456 | tf_op jit(solution)/shard_map/all_to_all | solution.py:282
  586.3 85.1 %all_to_all.41 = bf16[16,64,1536]{2,1,0:T(8,128)(2,1)S(1)} all-to-all(bf16[16,64,1536]{2,1,0:T(8,128)(2,1)S(1)} %get-tuple-element.505), channel_id=1, replica_groups=mesh['dp'=2,'expert'=16] {'expert'}, dimensions={0} | all-to-all | bytes 6291456 | tf_op jit(solution)/shard_map/all_to_all | solution.py:219
  683.1 52.7 %all-to-all-done.6 = bf16[16,64,1536]{2,1,0:T(8,128)(2,1)} async-done(((bf16[16,64,1536]{2,1,0:T(8,128)(2,1)}), bf16[16,64,1536]{2,1,0:T(8,128)(2,1)}, u32[]{:S(2)}, u32[]{:S(2)}) %all-to-all-start.6) | async-done | bytes 3145760 | tf_op jit(solution)/shard_map/all_to_all | solution.py:258
  746.9 14.0 all-to-all-start.3
  768.6 53.0 %all-to-all-done.3 = bf16[16,64,1536]{2,1,0:T(8,128)(2,1)S(1)} async-done(((bf16[16,64,1536]{2,1,0:T(8,128)(2,1)}), bf16[16,64,1536]{2,1,0:T(8,128)(2,1)S(1)}, u32[]{:S(2)}, u32[]{:S(2)}) %all-to-all-start.3) | async-done | bytes 3145760 | tf_op jit(solution)/shard_map/all_to_all | solution.py:226
  823.3 14.0 all-to-all-start.7
  861.4 36.6 %all-to-all-done.7 = bf16[16,64,1536]{2,1,0:T(8,128)(2,1)S(1)} async-done(((bf16[16,64,1536]{2,1,0:T(8,128)(2,1)}), bf16[16,64,1536]{2,1,0:T(8,128)(2,1)S(1)}, u32[]{:S(2)}, u32[]{:S(2)}) %all-to-all-start.7) | async-done | bytes 3145760 | tf_op jit(solution)/shard_map/all_to_all | solution.py:282
  913.3 34.7 %while.26 = (s32[]{:T(128)}, f32[64,8,3,64]{0,3,2,1:T(8,128)}, bf16[2,512,1024]{2,1,0:T(8,128)(2,1)}, s32[2]{0:T(128)S(1)}, bf16[1024,1024]{1,0:T(8,128)(2,1)}, ...) while((s32[]{:T(128)}, f32[64,8,3,64]{0,3,2,1:T(8,128)}, ...), condition=%wide.region_40.41_spmd.clone, body=%wide.region_39.40_spmd.clone.sunk | while | flops 515768896 | bytes 43980500 | solution.py:363
  954.0 31.5 %while.27 = (s32[]{:T(128)}, f32[64,8,3,64]{0,3,2,1:T(8,128)}, bf16[2,512,1024]{2,1,0:T(8,128)(2,1)}, s32[2]{0:T(128)S(1)}, bf16[1024,1024]{1,0:T(8,128)(2,1)}, ...) while((s32[]{:T(128)}, f32[64,8,3,64]{0,3,2,1:T(8,128)}, ...), condition=%wide.region_51.52_spmd.clone, body=%wide.region_50.51_spmd.clone.sunk | while | flops 515768896 | bytes 43194032 | solution.py:363
  1025.5 11.6 reduce-scatter.10.cloned.1.call-done
  1038.6 78.6 %reduce-scatter.12.cloned.1.call-done = bf16[64,1024]{1,0:T(8,128)(2,1)} async-done(((bf16[1024,1024]{1,0:T(8,128)(2,1)}), bf16[64,1024]{1,0:T(8,128)(2,1)}) %reduce-scatter.12.cloned.1.call-update) | async-done | bytes 131088 | tf_op jit(solution)/shard_map/reduce_scatter | solution.py:368
  1132.2 97.1 %reduce-scatter.22.cloned.1.call-done = f32[48,16]{1,0:T(8,128)} async-done(((f32[1536,16]{1,0:T(8,128)}), f32[48,16]{1,0:T(8,128)}) %reduce-scatter.22.cloned.1.call-update) | async-done | bytes 3088
  1257.3 40.7 %all-reduce.4 = (f32[1536]{0:T(1024)S(1)}, f32[1536]{0:T(1024)S(1)}) all-reduce(f32[1536]{0:T(1024)S(1)} %add.395, f32[1536]{0:T(1024)S(1)} %add.396), channel_id=7, replica_groups=mesh['dp'=2,'expert'=16] {'dp','expert'}, use_global_device_ids=true, to_apply=%region_59.60.clone | all-reduce | flops 3072 | bytes 24576
  1300.3 85.1 %reduce-scatter.16.cloned.1.call-done = f32[48,1536]{1,0:T(8,128)} async-done(((f32[1536,1536]{1,0:T(8,128)}), f32[48,1536]{1,0:T(8,128)}) %reduce-scatter.16.cloned.1.call-update) | async-done | bytes 294928 | tf_op jit(solution)/shard_map/reduce_scatter | solution.py:88
  1385.4 177.2 %reduce-scatter.14.cloned.1.call-done = f32[48,2560]{1,0:T(8,128)} async-done(((f32[1536,2560]{1,0:T(8,128)}), f32[48,2560]{1,0:T(8,128)}) %reduce-scatter.14.cloned.1.call-update) | async-done | bytes 491536 | tf_op jit(solution)/shard_map/reduce_scatter | solution.py:88
  (675 shorter events, 423.5 us)
Async XLA Ops:
  8.0 82.4 %all-gather.9.cloned.1.call-start = ((), (), s32[]{:S(2)}) async-start(), calls=%async_computation.15 | async-start | bytes 8110080 | tf_op jit(solution)/shard_map/all_gather | solution.py:64
  8.7 204.5 %all-gather.11.cloned.1.call-start = ((), (), s32[]{:S(2)}) async-start(), calls=%async_computation.16 | async-start | bytes 2228224 | tf_op jit(solution)/shard_map/all_gather | solution.py:160
  53.0 358.6 %copy-start.32 = (f32[1536]{0:T(1024)}, f32[1536]{0:T(1024)S(1)}, u32[]{:S(2)}) copy-start(f32[1536]{0:T(1024)S(1)} %convert_element_type.290) | copy-start | bytes 18436
  56.6 155.9 %copy-start.50 = (f32[64,32]{1,0:T(8,128)}, f32[64,32]{1,0:T(8,128)S(1)}, u32[]{:S(2)}) copy-start(f32[64,32]{1,0:T(8,128)S(1)} %get-tuple-element.509) | copy-start | bytes 24580
  95.3 116.1 %copy-start.36 = (bf16[2,64,1536]{2,1,0:T(8,128)(2,1)S(1)}, bf16[2,64,1536]{2,1,0:T(8,128)(2,1)}, u32[]{:S(2)}) copy-start(bf16[2,64,1536]{2,1,0:T(8,128)(2,1)} %param.17) | copy-start | bytes 1179652
  96.6 127.8 %all-gather.13.cloned.1.call-start = ((), (), s32[]{:S(2)}) async-start(), calls=%async_computation.17 | async-start | bytes 4866048 | tf_op jit(solution)/shard_map/all_gather | solution.py:65
  136.5 431.2 %copy-start.74 = (f32[1536]{0:T(1024)}, f32[1536]{0:T(1024)S(1)}, u32[]{:S(2)}) copy-start(f32[1536]{0:T(1024)S(1)} %convert_element_type.299) | copy-start | bytes 18436
  321.2 64.6 %all-to-all-start.4 = ((bf16[16,64,1536]{2,1,0:T(8,128)(2,1)}), bf16[16,64,1536]{2,1,0:T(8,128)(2,1)}, u32[]{:S(2)}, u32[]{:S(2)}) async-start(bf16[16,64,1536]{2,1,0:T(8,128)(2,1)} %get-tuple-element.502), calls=%async_computation.4 | async-start | bytes 6291456 | tf_op jit(solution)/shard_map/all_to_all | solution.py:258
  325.7 15.3 all-gather.15.cloned.1.call-start
  326.3 27.0 %all-gather.17.cloned.1.call-start = ((), (), s32[]{:S(2)}) async-start(), calls=%async_computation.19 | async-start | bytes 2359296 | tf_op jit(solution)/shard_map/all_gather | solution.py:82
  396.9 82.1 %all-to-all-start.1 = ((bf16[16,64,1536]{2,1,0:T(8,128)(2,1)}), bf16[16,64,1536]{2,1,0:T(8,128)(2,1)S(1)}, u32[]{:S(2)}, u32[]{:S(2)}) async-start(bf16[16,64,1536]{2,1,0:T(8,128)(2,1)} %bitcast.631), calls=%async_computation.1 | async-start | bytes 6291456 | tf_op jit(solution)/shard_map/all_to_all | solution.py:226
  410.9 116.3 %all-gather.19.cloned.1.call-start = ((), (), s32[]{:S(2)}) async-start(), calls=%async_computation.20 | async-start | bytes 2228224 | tf_op jit(solution)/shard_map/all_gather | solution.py:160
  479.0 81.5 %all-to-all-start.5 = ((bf16[16,64,1536]{2,1,0:T(8,128)(2,1)}), bf16[16,64,1536]{2,1,0:T(8,128)(2,1)}, u32[]{:S(2)}, u32[]{:S(2)}) async-start(bf16[16,64,1536]{2,1,0:T(8,128)(2,1)} %bitcast.629), calls=%async_computation.5 | async-start | bytes 6291456 | tf_op jit(solution)/shard_map/all_to_all | solution.py:282
  671.3 64.4 %all-to-all-start.6 = ((bf16[16,64,1536]{2,1,0:T(8,128)(2,1)}), bf16[16,64,1536]{2,1,0:T(8,128)(2,1)}, u32[]{:S(2)}, u32[]{:S(2)}) async-start(bf16[16,64,1536]{2,1,0:T(8,128)(2,1)} %get-tuple-element.504), calls=%async_computation.7 | async-start | bytes 6291456 | tf_op jit(solution)/shard_map/all_to_all | solution.py:258
  746.9 74.7 %all-to-all-start.3 = ((bf16[16,64,1536]{2,1,0:T(8,128)(2,1)}), bf16[16,64,1536]{2,1,0:T(8,128)(2,1)S(1)}, u32[]{:S(2)}, u32[]{:S(2)}) async-start(bf16[16,64,1536]{2,1,0:T(8,128)(2,1)} %bitcast.632), calls=%async_computation.3 | async-start | bytes 6291456 | tf_op jit(solution)/shard_map/all_to_all | solution.py:226
  823.3 74.7 %all-to-all-start.7 = ((bf16[16,64,1536]{2,1,0:T(8,128)(2,1)}), bf16[16,64,1536]{2,1,0:T(8,128)(2,1)S(1)}, u32[]{:S(2)}, u32[]{:S(2)}) async-start(bf16[16,64,1536]{2,1,0:T(8,128)(2,1)} %bitcast.630), calls=%async_computation.8 | async-start | bytes 6291456 | tf_op jit(solution)/shard_map/all_to_all | solution.py:282
  837.4 199.8 %reduce-scatter.10.cloned.1.call-start = ((), (), s32[]{:S(2)}) async-start(), calls=%async_computation.21 | async-start | bytes 2228224 | tf_op jit(solution)/shard_map/reduce_scatter | solution.py:368
  948.0 169.1 %reduce-scatter.12.cloned.1.call-start = ((), (), s32[]{:S(2)}) async-start(), calls=%async_computation.22 | async-start | bytes 2228224 | tf_op jit(solution)/shard_map/reduce_scatter | solution.py:368
  985.5 143.3 %reduce-scatter.20.cloned.1.call-start = ((), (), s32[]{:S(2)}) async-start(), calls=%async_computation.26 | async-start | bytes 2359296 | tf_op jit(solution)/shard_map/reduce_scatter | solution.py:94
  994.8 234.5 %reduce-scatter.22.cloned.1.call-start = ((), (), s32[]{:S(2)}) async-start(), calls=%async_computation.27 | async-start | bytes 811008
  1003.4 238.8 %reduce-scatter.18.cloned.1.call-start = ((), (), s32[]{:S(2)}) async-start(), calls=%async_computation.25 | async-start | bytes 4718592 | tf_op jit(solution)/shard_map/reduce_scatter | solution.py:94
  1013.0 372.4 %reduce-scatter.16.cloned.1.call-start = ((), (), s32[]{:S(2)}) async-start(), calls=%async_computation.24 | async-start | bytes 9732096 | tf_op jit(solution)/shard_map/reduce_scatter | solution.py:88
  1020.7 541.9 %reduce-scatter.14.cloned.1.call-start = ((), (), s32[]{:S(2)}) async-start(), calls=%async_computation.23 | async-start | bytes 16220160 | tf_op jit(solution)/shard_map/reduce_scatter | solution.py:88
  1025.0 93.6 %copy-start.12 = (bf16[2,64,1536]{2,1,0:T(8,128)(2,1)S(1)}, bf16[2,64,1536]{2,1,0:T(8,128)(2,1)}, u32[]{:S(2)}) copy-start(bf16[2,64,1536]{2,1,0:T(8,128)(2,1)} %param.16) | copy-start | bytes 1179652
  (164 other events, 1351.0 us)
Sparse Core Ops, SparseCore 0:
  11.7 78.6 all-gather.8
  96.7 59.4 all-gather.10
  159.1 62.6 all-gather.12
  424.9 96.8 all-gather.18
  948.1 88.9 reduce-scatter.9
  1039.3 77.8 reduce-scatter.11
  1120.0 6.1 reduce-scatter.19
  1132.6 96.6 reduce-scatter.21
  1232.2 9.9 reduce-scatter.17
  1248.5 136.8 reduce-scatter.15
  1393.0 169.5 reduce-scatter.13
Sparse Core Ops, SparseCore 1:
  327.8 13.2 all-gather.14
  342.4 10.9 all-gather.16
where the time goes:
time: 1580 us; the launch traced here: 1570 us
  waiting for transfers between devices  736 us (47%)
  blocking collectives  346 us (22%)
  matrix products  180 us (11%)
  local copies, waits for them, and re-layouts  138 us (9%)
  other arithmetic  75.5 us (5%)
  starting transfers between devices  74 us (5%)
  between operations  17.6 us (1%)
    reduce_scatter x2, waiting for transfers between devices, reduce_dense(): lax.psum_scatter(grad_terms, ('dp', 'expert'), scatter_dimension=0, tiled...  262 us
    all_to_all x2, blocking collectives, on_device(): lax.all_to_all(outgoing, 'expert', split_axis=0, concat_axis=0, tiled=True)  160 us
    unnamed x14, waiting for transfers between devices  99.4 us
    all_to_all x2, waiting for transfers between devices, on_device(): lax.all_to_all(result.reshape(sources, slot_count, model_width), 'expert'...  97.3 us
    reduce_scatter x2, waiting for transfers between devices, on_device(): lax.psum_scatter(grad_key_value.reshape(key_total, 2 * key_width).astype(...  90.2 us
    all_to_all x2, waiting for transfers between devices, on_device(): lax.all_to_all(grad_outgoing, 'expert', split_axis=0, concat_axis=0, tile...  85.2 us
    unnamed x2, blocking collectives  83.2 us
    all_gather x1, blocking collectives, gather_dense(): lax.all_gather(w_router, ('dp', 'expert'), axis=0, tiled=True)  64.5 us
  transfers between devices with their start and end apart: 19, of which 15 were waited for; matrix products, arithmetic and copies ran while one was open for 17% of the time, Pallas kernels for 0%

commit v1 on v0

v1 whole, which is shorter than its diff:
```python
import math

import jax
import jax.numpy as jnp
from jax import lax
from jax.experimental import pallas as pl
from jax.experimental.pallas import tpu as pltpu
from jax.sharding import Mesh
from jax.sharding import PartitionSpec as P

HEADS = 24
KV_HEADS = 8
HEAD_DIM = 64
EXP_FF = 512
TOP = 8

epsilon = 1e-06
rope_base = 10000.0
masked = -1e30

GROUP = HEADS // KV_HEADS
HALF = HEAD_DIM // 2
LANES = 128
SLAB = 3 * LANES
META_ROWS = 16
BLOCK = 256
SWAP = [(0, 1), (1, 0)]
bf16 = jnp.bfloat16
f32 = jnp.float32


def dot(a, b, da, db):
    return lax.dot_general(a, b, (((da,), (db,)), ((), ())), preferred_element_type=f32)


def gather_bits(x, order, every):
    have = []
    for axis in order:
        other = lax.ppermute(x, axis, SWAP)
        place = sum(every.index(h) < every.index(axis) for h in have)
        first = lax.axis_index(axis) == 0
        x = jnp.stack([jnp.where(first, x, other), jnp.where(first, other, x)], place)
        have.append(axis)
    return x


def scatter_bits(x, order, every):
    left = list(every)
    for axis in order:
        place = left.index(axis)
        mine = lax.axis_index(axis)
        keep = lax.dynamic_index_in_dim(x, mine, place, keepdims=False)
        send = lax.dynamic_index_in_dim(x, 1 - mine, place, keepdims=False)
        other = lax.ppermute(send.astype(bf16), axis, SWAP)
        left.pop(place)
        x = keep.astype(f32) + other.astype(f32)
        if left:
            x = x.astype(bf16)
    return x


def project_kernel(a_ref, b_ref, gain_ref, w_ref, cos_ref, sin_ref, low_ref, q_ref, k_ref, v_ref):
    step = pl.program_id(0)
    half = pl.num_programs(0) // 2

    def work(x_ref):
        x = x_ref[...].astype(f32)
        r = lax.rsqrt(jnp.mean(x * x, -1, keepdims=True) + epsilon)
        low = (x * r * gain_ref[...]).astype(bf16)
        low_ref[...] = low
        p = dot(low, w_ref[...], 1, 0)
        lane = lax.broadcasted_iota(jnp.int32, (x.shape[0], LANES), 1)
        u, w = p[:, :LANES], p[:, LANES : 2 * LANES]
        v = jnp.where(lane < HEAD_DIM, p[:, 2 * LANES :], 0.0)
        c, s = cos_ref[...], sin_ref[...]
        for at, turned in ((0, u * c - w * s), (LANES, w * c + u * s)):
            key = jnp.where(lane >= GROUP * HALF, turned, 0.0)
            key = pltpu.roll(key, HALF, 1) + pltpu.roll(key, 2 * HALF, 1) + pltpu.roll(key, 3 * HALF, 1)
            k_ref[:, at : at + LANES] = key.astype(bf16)
            for h in range(GROUP):
                q_ref[h, :, at : at + LANES] = jnp.where(lane // HALF == h, turned, 0.0).astype(bf16)
        zero = jnp.zeros(v.shape, bf16)
        first, second = v.astype(bf16), pltpu.roll(v, HEAD_DIM, 1).astype(bf16)
        for h in range(GROUP):
            for at in range(2):
                part = zero if h // 2 != at else (first if h % 2 == 0 else second)
                v_ref[h, :, at * LANES : (at + 1) * LANES] = part

    pl.when(step < half)(lambda: work(a_ref))
    pl.when(step >= half)(lambda: work(b_ref))


def project(part_a, part_b, gain, w_slab, cosine, sine):
    rows, width = part_a.shape
    length = 2 * rows
    steps = length // BLOCK
    half = steps // 2
    wide = 2 * LANES
    row = lambda cols: pl.BlockSpec((BLOCK, cols), lambda i: (i, 0))
    heads = pl.BlockSpec((GROUP, BLOCK, wide), lambda i: (0, i, 0))
    return pl.pallas_call(
        project_kernel,
        grid=(steps,),
        in_specs=[
            pl.BlockSpec((BLOCK, width), lambda i: (jnp.minimum(i, half - 1), 0)),
            pl.BlockSpec((BLOCK, width), lambda i: (jnp.maximum(i - half, 0), 0)),
            pl.BlockSpec((1, width), lambda i: (0, 0)),
            pl.BlockSpec((width, SLAB), lambda i: (0, 0)),
            row(LANES),
            row(LANES),
        ],
        out_specs=[row(width), heads, row(wide), heads],
        out_shape=[
            jax.ShapeDtypeStruct((length, width), bf16),
            jax.ShapeDtypeStruct((GROUP, length, wide), bf16),
            jax.ShapeDtypeStruct((length, wide), bf16),
            jax.ShapeDtypeStruct((GROUP, length, wide), bf16),
        ],
        compiler_params=pltpu.CompilerParams(vmem_limit_bytes=40 * 2**20),
        cost_estimate=pl.CostEstimate(
            flops=2 * length * width * SLAB, bytes_accessed=12 * 2**20, transcendentals=length
        ),
    )(part_a, part_b, gain, w_slab, cosine, sine)


def allowed_block(col_ref, row_ref, start, width):
    shape = (BLOCK, width)
    places = start + lax.broadcasted_iota(jnp.int32, shape, 0)
    keys = lax.broadcasted_iota(jnp.int32, shape, 1)
    same = col_ref[start : start + BLOCK, :] == row_ref[:, :width]
    return same & (keys <= places)


def attend_kernel(q_ref, k_ref, v_ref, col_ref, row_ref, o_ref, lse_ref):
    lane = lax.broadcasted_iota(jnp.int32, (BLOCK, LANES), 1)
    for start in range(0, k_ref.shape[0], BLOCK):
        width = start + BLOCK
        rows = slice(start, width)
        allowed = allowed_block(col_ref, row_ref, start, width)
        total = jnp.zeros((BLOCK, 2 * LANES), f32)
        logs = jnp.zeros((BLOCK, LANES), f32)
        for h in range(GROUP):
            s = dot(q_ref[h, rows, :], k_ref[:width, :], 1, 1) * 0.125
            s = jnp.where(allowed, s, masked)
            top = jnp.max(s, -1, keepdims=True)
            p = jnp.exp(s - top)
            below = jnp.sum(p, -1, keepdims=True)
            total = total + dot((p / below).astype(bf16), v_ref[h, :width, :], 1, 0)
            logs = jnp.where(lane == h, top + jnp.log(below), logs)
        o_ref[rows, :] = total.astype(bf16)
        lse_ref[rows, :] = logs


def attend(q, k, v, docs_col, docs_row):
    length, wide = k.shape
    return pl.pallas_call(
        attend_kernel,
        out_shape=[
            jax.ShapeDtypeStruct((length, wide), bf16),
            jax.ShapeDtypeStruct((length, LANES), f32),
        ],
        compiler_params=pltpu.CompilerParams(vmem_limit_bytes=48 * 2**20),
        cost_estimate=pl.CostEstimate(
            flops=2 * GROUP * length * length * wide,
            bytes_accessed=8 * 2**20,
            transcendentals=GROUP * length * length // 2,
        ),
    )(q, k, v, docs_col, docs_row)


def attend_back_kernel(
    q_ref, k_ref, v_ref, g_ref, lse_ref, col_ref, row_ref, cos_ref, sin_ref, out_ref, dk_ref, dv_ref
):
    length = k_ref.shape[0]
    wide = 2 * LANES
    dk_ref[...] = jnp.zeros_like(dk_ref)
    dv_ref[...] = jnp.zeros_like(dv_ref)
    lane = lax.broadcasted_iota(jnp.int32, (BLOCK, LANES), 1)
    wide_lane = lax.broadcasted_iota(jnp.int32, (BLOCK, wide), 1)
    for start in range(0, length, BLOCK):
        width = start + BLOCK
        rows = slice(start, width)
        allowed = allowed_block(col_ref, row_ref, start, width)
        dq = jnp.zeros((BLOCK, wide), f32)
        grads = g_ref[rows, :].astype(f32)
        for h in range(GROUP):
            q = q_ref[h, rows, :]
            lse = jnp.sum(jnp.where(lane == h, lse_ref[rows, :], 0.0), -1, keepdims=True)
            s = dot(q, k_ref[:width, :], 1, 1) * 0.125
            p = jnp.where(allowed, jnp.exp(jnp.where(allowed, s, masked) - lse), 0.0)
            g = jnp.where(wide_lane // HEAD_DIM == h, grads, 0.0).astype(bf16)
            dp = dot(g, v_ref[h, :width, :], 1, 1)
            delta = jnp.sum(p * dp, -1, keepdims=True)
            ds = (p * (dp - delta)).astype(bf16)
            part = dot(ds, k_ref[:width, :], 1, 0)
            dq = dq + jnp.where(wide_lane % LANES // HALF == h, part, 0.0)
            dk_ref[:width, :] += dot(ds, q, 0, 0)
            dv_ref[:width, :] += dot(p.astype(bf16), g, 0, 0)
        out_ref[rows, :LANES] = dq[:, :LANES].astype(out_ref.dtype)
        out_ref[rows, LANES:wide] = dq[:, LANES:].astype(out_ref.dtype)
    for start in range(0, length, BLOCK):
        rows = slice(start, start + BLOCK)
        halves = []
        for at in (0, LANES):
            key = dk_ref[rows, at : at + LANES]
            key = pltpu.roll(key, 3 * HALF, 1) + pltpu.roll(key, 2 * HALF, 1) + pltpu.roll(key, HALF, 1)
            both = jnp.where(lane >= GROUP * HALF, key, out_ref[rows, at : at + LANES])
            halves.append(both * 0.125)
        c, s = cos_ref[rows, :], sin_ref[rows, :]
        u, w = halves
        out_ref[rows, :LANES] = u * c + w * s
        out_ref[rows, LANES:wide] = w * c - u * s
        v = dv_ref[rows, :LANES] + dv_ref[rows, LANES:]
        v = v + pltpu.roll(v, HEAD_DIM, 1)
        out_ref[rows, wide:] = jnp.where(lane < HEAD_DIM, v, 0.0)


def attend_back_entry(*refs):
    *ins, out_ref, full_ref, dk_ref, dv_ref = refs
    attend_back_kernel(*ins, full_ref, dk_ref, dv_ref)
    out_ref[...] = full_ref[...].astype(bf16)


def attend_back(q, k, v, g, lse, docs_col, docs_row, cosine, sine):
    length, wide = k.shape
    return pl.pallas_call(
        attend_back_entry,
        out_shape=jax.ShapeDtypeStruct((length, SLAB), bf16),
        scratch_shapes=[
            pltpu.VMEM((length, SLAB), f32),
            pltpu.VMEM((length, wide), f32),
            pltpu.VMEM((length, wide), f32),
        ],
        compiler_params=pltpu.CompilerParams(vmem_limit_bytes=52 * 2**20),
        cost_estimate=pl.CostEstimate(
            flops=5 * GROUP * length * length * wide,
            bytes_accessed=8 * 2**20,
            transcendentals=GROUP * length * length // 2,
        ),
    )(q, k, v, g, lse, docs_col, docs_row, cosine, sine)


def split_columns(w_qkv):
    rows = w_qkv.shape[0]
    q_width, k_width = HEADS * HEAD_DIM, KV_HEADS * HEAD_DIM
    q = w_qkv[:, :q_width].reshape(rows, KV_HEADS, GROUP, 2, HALF)
    k = w_qkv[:, q_width : q_width + k_width].reshape(rows, KV_HEADS, 1, 2, HALF)
    both = jnp.concatenate([q, k], 2)
    return (
        both[:, :, :, 0].reshape(rows, KV_HEADS, LANES),
        both[:, :, :, 1].reshape(rows, KV_HEADS, LANES),
        w_qkv[:, q_width + k_width :].reshape(rows, KV_HEADS, HEAD_DIM),
    )


def join_columns(u, w, v):
    rows = u.shape[0]
    both = jnp.stack(
        [u.reshape(rows, KV_HEADS, GROUP + 1, HALF), w.reshape(rows, KV_HEADS, GROUP + 1, HALF)], 3
    )
    return jnp.concatenate(
        [
            both[:, :, :GROUP].reshape(rows, HEADS * HEAD_DIM),
            both[:, :, GROUP:].reshape(rows, KV_HEADS * HEAD_DIM),
            v.reshape(rows, KV_HEADS * HEAD_DIM),
        ],
        1,
    )


def halves(x):
    high = lax.reduce_precision(x, 8, 7)
    return high.astype(bf16), (x - high).astype(bf16)


def on_device(
    dp_axes,
    ex_axes,
    tokens,
    cotangent,
    segments,
    positions,
    routes,
    w_qkv,
    w_out,
    w_router,
    norm_attn,
    norm_ffn,
    w_gate_up,
    w_down,
):
    batches, local, width = tokens.shape
    experts = w_router.shape[1]
    count = 2 ** len(ex_axes)
    length = count * local
    units = batches * KV_HEADS
    parts = count // units
    shard = w_qkv.shape[0]
    rows = batches * local
    me = lax.axis_index(ex_axes)
    bit = lambda b: ex_axes[len(ex_axes) - 1 - b]
    pair_axis = bit(2)
    token_axes = tuple(a for a in ex_axes if a != pair_axis)
    far = token_axes[:-2]
    orders = (far + (bit(0), bit(1)), far + (bit(1), bit(0)))

    u_cols, w_cols, v_cols = split_columns(w_qkv)
    small = jnp.concatenate([norm_attn[:, None], norm_ffn[:, None], w_router], 1)
    small = jnp.pad(small, ((0, 0), (0, SLAB - 2 * LANES - HEAD_DIM - small.shape[1])))
    small = jnp.broadcast_to(small[:, None, :], (shard, KV_HEADS, small.shape[1]))
    slab = jnp.transpose(jnp.concatenate([u_cols, w_cols, v_cols, small], -1), (1, 0, 2))
    meta = jnp.stack([segments, positions // 64, positions % 64], 1).astype(bf16)
    meta = jnp.pad(meta, ((0, 0), (0, META_ROWS - 3), (0, SLAB - local)))
    payload = jnp.concatenate(
        [
            jnp.broadcast_to(slab[None], (batches,) + slab.shape),
            jnp.broadcast_to(meta[:, None], (batches, KV_HEADS) + meta.shape[1:]),
        ],
        2,
    ).reshape(units, shard + META_ROWS, SLAB)
    payload = jnp.concatenate([payload] * parts, 0)
    arrived = lax.all_to_all(payload, ex_axes, 0, 0, tiled=True)
    w_slab = gather_bits(arrived[:, :shard].reshape(count * shard, SLAB), dp_axes, dp_axes)
    w_slab = w_slab.reshape(width, SLAB)
    extra_at = 2 * LANES + HEAD_DIM
    gain_attn = w_slab[:, extra_at].astype(f32)
    gain_ffn = w_slab[:, extra_at + 1].astype(f32)
    router_full = w_slab[:, extra_at + 2 : extra_at + 2 + experts]
    info = arrived[:, shard : shard + 3, :local].astype(jnp.int32)
    docs = info[:, 0].reshape(length)
    places = (info[:, 1] * 64 + info[:, 2]).reshape(length)
    frequency = rope_base ** (-jnp.arange(HALF, dtype=f32) / HALF)
    angles = places.astype(f32)[:, None] * jnp.tile(frequency, GROUP + 1)[None, :]
    cosine, sine = jnp.cos(angles), jnp.sin(angles)
    docs_col, docs_row = docs[:, None], docs[None, :]

    mb_axis = bit(3)
    mine = lax.axis_index(mb_axis)
    own = lax.dynamic_index_in_dim(tokens, mine, 0, keepdims=False)
    other = lax.ppermute(
        lax.dynamic_index_in_dim(tokens, 1 - mine, 0, keepdims=False), mb_axis, SWAP
    )
    first = mine == 0
    group = jnp.stack([jnp.where(first, own, other), jnp.where(first, other, own)], 0)
    middle = tuple(a for a in ex_axes[:-2] if a != mb_axis)
    group = gather_bits(group, middle, middle)
    group = jnp.moveaxis(group, len(middle), 0)
    sides = []
    for part, last in ((group[0], (bit(0), bit(1))), (group[1], (bit(1), bit(0)))):
        pair = gather_bits(part, last, (bit(1), bit(0)))
        sides.append(jnp.moveaxis(pair, (0, 1), (len(middle), len(middle) + 1)))
    if len(middle) == 1:
        sides = [s.reshape(length // 2, width) for s in sides]
    else:
        at = ex_axes.index(mb_axis)
        whole = jnp.stack(sides, at).reshape(length, width)
        sides = [whole[: length // 2], whole[length // 2 :]]

    out_full = lax.all_gather(w_out, dp_axes + ex_axes, axis=0, tiled=True)
    grad_rows = [
        lax.all_gather(cotangent[m], token_axes, axis=0, tiled=True) for m in range(batches)
    ]
    qkv_mixed = jnp.concatenate([p.reshape(shard, -1) for p in (u_cols, w_cols, v_cols)], 1)
    qkv_full = lax.all_gather(qkv_mixed, dp_axes + ex_axes, axis=0, tiled=True)

    gu_shard, down_shard = w_gate_up[0], w_down[0]
    gu_other = lax.ppermute(gu_shard, pair_axis, SWAP)
    down_other = lax.ppermute(down_shard, pair_axis, SWAP)
    full = lambda s: gather_bits(s, dp_axes, dp_axes).reshape(-1, s.shape[1])
    gate_ups = [full(gu_shard), full(gu_other)]
    downs = [full(down_shard), full(down_other)]

    first_low, q, k, v = project(*sides, gain_attn[None, :], w_slab, cosine, sine)
    attended, lse = attend(q, k, v, docs_col, docs_row)
    back = lax.all_to_all(attended.reshape(count, local, 2 * LANES), ex_axes, 0, 0, tiled=True)
    head_width = GROUP * HEAD_DIM
    attended_low = (
        back[:units, :, :head_width]
        .reshape(batches, KV_HEADS, local, head_width)
        .transpose(0, 2, 1, 3)
        .reshape(rows, HEADS * HEAD_DIM)
    )
    x = tokens.reshape(rows, width).astype(f32)
    g = cotangent.reshape(rows, width).astype(f32)
    y_one = x + dot(attended_low, out_full, 1, 1)
    r_two = lax.rsqrt(jnp.mean(y_one * y_one, -1, keepdims=True) + epsilon)
    n_two = y_one * r_two
    second_low = (n_two * gain_ffn).astype(bf16)
    logits = dot(second_low, router_full, 1, 0)
    raised = jnp.exp(logits - jnp.max(logits, -1, keepdims=True))
    router = raised / jnp.sum(raised, -1, keepdims=True)
    numbers = jnp.arange(experts, dtype=jnp.int32)
    chosen = jnp.sum(
        (routes.reshape(rows, TOP)[:, :, None] == numbers[None, None, :]).astype(f32), 1
    )
    pick_total = jnp.sum(chosen * router, -1, keepdims=True)
    gates = chosen * router / pick_total
    tail = LANES - 2 * experts
    sent = jnp.concatenate([second_low, *halves(gates), jnp.zeros((rows, tail), bf16)], 1)
    sent = sent.reshape(batches, local, width + LANES)

    mixtures, grad_inputs, keeps = [], [], []
    for m in range(batches):
        got = gather_bits(sent[m], orders[m % 2], token_axes).reshape(-1, width + LANES)
        seen = got[:, :width]
        gate_high = got[:, width : width + experts].astype(f32)
        gate_low = got[:, width + experts : width + 2 * experts].astype(f32)
        all_gates = gate_high + gate_low
        grads = grad_rows[m]
        pairs, weighted, gate_grads = [], [], jnp.zeros(all_gates.shape, f32)
        for j, expert in enumerate((me, me ^ 4)):
            is_mine = numbers[None, :] == expert
            share = jnp.sum(jnp.where(is_mine, all_gates, 0.0), -1, keepdims=True)
            gate_up = dot(seen, gate_ups[j], 1, 0)
            gate, up = gate_up[:, :EXP_FF], gate_up[:, EXP_FF:]
            sg = 1.0 / (1.0 + jnp.exp(-gate))
            hidden = (gate * sg * up).astype(bf16).astype(f32)
            grad_plain = dot(grads, downs[j], 1, 1)
            gate_grad = jnp.sum(grad_plain * hidden, -1, keepdims=True)
            gate_grads = gate_grads + jnp.where(is_mine, gate_grad, 0.0)
            grad_hidden = share * grad_plain
            weighted.append((share * hidden).astype(bf16))
            pairs.append(
                jnp.concatenate(
                    [grad_hidden * up * sg * (1.0 + gate * (1.0 - sg)), grad_hidden * gate * sg], 1
                ).astype(bf16)
            )
        grad_in = dot(pairs[0], gate_ups[0], 1, 1) + dot(pairs[1], gate_ups[1], 1, 1)
        grad_in = jnp.concatenate(
            [grad_in.astype(bf16), *halves(gate_grads), jnp.zeros((seen.shape[0], tail), bf16)], 1
        ).reshape((2,) * len(token_axes) + (local, width + LANES))
        grad_inputs.append(scatter_bits(grad_in, orders[m % 2][::-1], token_axes))
        mixture = dot(weighted[0], downs[0], 1, 0) + dot(weighted[1], downs[1], 1, 0)
        mixtures.append(
            lax.psum_scatter(mixture.astype(bf16), token_axes, scatter_dimension=0, tiled=True)
        )
        keeps.append((seen, grads, pairs, weighted))

    grad_experts = []
    for j in range(2):
        grad_gu = sum(dot(seen, pairs[j], 0, 0) for seen, _, pairs, _ in keeps)
        grad_dn = sum(dot(weighted[j], grads, 0, 0) for _, grads, _, weighted in keeps)
        shape = (2,) * len(dp_axes)
        grad_experts.append(
            tuple(
                scatter_bits(t.reshape(shape + (-1, t.shape[1])), dp_axes, dp_axes)
                for t in (grad_gu, grad_dn)
            )
        )
    grad_gate_up, grad_down = (
        mine_part + lax.ppermute(theirs.astype(bf16), pair_axis, SWAP).astype(f32)
        for mine_part, theirs in zip(*grad_experts)
    )
    mixed = y_one + jnp.stack(mixtures).reshape(rows, width).astype(f32)

    came = jnp.stack(grad_inputs).reshape(rows, width + LANES)
    grad_gates = came[:, width : width + experts] + came[:, width + experts : width + 2 * experts]
    grad_gates = chosen * grad_gates
    grad_picked = (
        chosen * (grad_gates - jnp.sum(grad_gates * gates, -1, keepdims=True)) / pick_total
    )
    grad_logits = (
        router * (grad_picked - jnp.sum(router * grad_picked, -1, keepdims=True))
    ).astype(bf16)
    grad_router = dot(second_low, grad_logits, 0, 0)
    grad_second = came[:, :width] + dot(grad_logits, router_full, 1, 1)
    c_two = grad_second * gain_ffn
    grad_y = g + r_two * (c_two - n_two * jnp.mean(c_two * n_two, -1, keepdims=True))
    grad_gain_ffn = jnp.sum(grad_second * n_two, 0)
    grad_branch = grad_y.astype(bf16)
    grad_attended = dot(grad_branch, out_full, 1, 0).astype(bf16)
    payload = jnp.pad(
        grad_attended.reshape(batches, local, KV_HEADS, head_width).transpose(0, 2, 1, 3),
        ((0, 0), (0, 0), (0, 0), (0, 2 * LANES - head_width)),
    ).reshape(units, local, 2 * LANES)
    payload = jnp.concatenate([payload] * parts, 0)
    grad_heads = lax.all_to_all(payload, ex_axes, 0, 0, tiled=True).reshape(length, 2 * LANES)

    grad_out = dot(grad_branch, attended_low, 0, 0)
    extras = jnp.concatenate([grad_router, grad_gain_ffn[:, None]], 1)
    extras = jnp.pad(extras, ((0, 0), (0, LANES - extras.shape[1])))
    dense = jnp.concatenate([grad_out, extras], 1).astype(bf16)
    dense = scatter_bits(
        dense.reshape((2,) * len(dp_axes) + (-1, dense.shape[1])), dp_axes, dp_axes
    )
    dense = lax.psum_scatter(dense.astype(bf16), ex_axes, scatter_dimension=0, tiled=True)
    dense = dense.astype(f32)

    grad_proj = attend_back(q, k, v, grad_heads, lse, docs_col, docs_row, cosine, sine)
    back = lax.all_to_all(grad_proj.reshape(count, local, SLAB), ex_axes, 0, 0, tiled=True)
    back = back[:units].reshape(batches, KV_HEADS, local, SLAB).transpose(0, 2, 1, 3)
    back = jnp.concatenate(
        [
            back[..., :LANES].reshape(rows, -1),
            back[..., LANES : 2 * LANES].reshape(rows, -1),
            back[..., 2 * LANES : 2 * LANES + HEAD_DIM].reshape(rows, -1),
        ],
        1,
    )
    grad_first = dot(back, qkv_full, 1, 1)
    grad_slab = dot(first_low, grad_proj, 0, 0)
    grad_slab = scatter_bits(
        grad_slab.reshape((2,) * len(dp_axes) + (-1, SLAB)), dp_axes, dp_axes
    )
    grad_slab = lax.all_to_all(
        grad_slab.astype(bf16).reshape(count, shard, SLAB), ex_axes, 0, 0, tiled=True
    )
    grad_slab = jnp.sum(
        grad_slab[:units].reshape(batches, KV_HEADS, shard, SLAB).astype(f32), 0
    ).transpose(1, 0, 2)
    grad_qkv = join_columns(
        grad_slab[..., :LANES],
        grad_slab[..., LANES : 2 * LANES],
        grad_slab[..., 2 * LANES : 2 * LANES + HEAD_DIM],
    )
    grad_gain_attn = jnp.sum(grad_qkv * w_qkv.astype(f32), -1) / norm_attn.astype(f32)
    r_one = lax.rsqrt(jnp.mean(x * x, -1, keepdims=True) + epsilon)
    n_one = x * r_one
    c_one = grad_first * gain_attn
    grad_tokens = grad_y + r_one * (c_one - n_one * jnp.mean(c_one * n_one, -1, keepdims=True))

    out_width = HEADS * HEAD_DIM
    return (
        mixed.astype(bf16).reshape(tokens.shape),
        grad_tokens.reshape(tokens.shape),
        grad_qkv,
        dense[:, :out_width],
        dense[:, out_width : out_width + experts],
        grad_gain_attn,
        dense[:, out_width + experts],
        grad_gate_up[None],
        grad_down[None],
    )


def solution(mesh):
    dp_bits = int(math.log2(mesh.shape["dp"]))
    ex_bits = int(math.log2(mesh.shape["expert"]))
    dp_axes = tuple(f"d{b}" for b in reversed(range(dp_bits)))
    ex_axes = tuple(f"e{b}" for b in reversed(range(ex_bits)))
    cube = Mesh(mesh.devices.reshape((2,) * (dp_bits + ex_bits)), dp_axes + ex_axes)
    every = dp_axes + ex_axes
    by_tokens = P(None, every, None)

    def run(*arrays):
        return on_device(dp_axes, ex_axes, *arrays)

    return jax.shard_map(
        run,
        mesh=cube,
        in_specs=(
            by_tokens,
            by_tokens,
            P(None, every),
            P(None, every),
            by_tokens,
            P(every, None),
            P(every, None),
            P(every, None),
            P(every),
            P(every),
            P(ex_axes, dp_axes, None),
            P(ex_axes, dp_axes, None),
        ),
        out_specs=(
            by_tokens,
            by_tokens,
            P(every, None),
            P(every, None),
            P(every, None),
            P(every),
            P(every),
            P(ex_axes, dp_axes, None),
            P(ex_axes, dp_axes, None),
        ),
        check_vma=False,
    )
```

time: 1580 us -> 658 us (0.42)
  waiting for transfers between devices: 736 us -> 338 us
  blocking collectives: 346 us -> 0 us
  matrix products: 180 us -> 85.4 us
  local copies, waits for them, and re-layouts: 138 us -> 63.9 us
  Pallas kernels: 0 us -> 23.1 us
    reduce_scatter x6 -> x3, waiting for transfers between devices: 364 us -> 66.7 us  [the longest x1 66.6 us: on_device(): lax.psum_scatter(dense.astype(bf16), ex_axes, scatter_dimension=0, tiled=...]
    ppermute x0 -> x33, waiting for transfers between devices: none -> 185 us  [the longest x16 74.7 us: gather_bits(): other = lax.ppermute(x, axis, SWAP)]
    all_to_all x2 -> x0, blocking collectives: 160 us -> none  [on_device(): lax.all_to_all(outgoing, 'expert', split_axis=0, concat_axis=0, tiled=True)]
    all_to_all x6 -> x5, waiting for transfers between devices: 220 us -> 85.3 us  [the longest x1 56 us: on_device(): lax.all_to_all(payload, ex_axes, 0, 0, tiled=True)]
    all_gather x2 -> x0, blocking collectives: 103 us -> none  [the longest x1 64.5 us: gather_dense(): lax.all_gather(w_router, ('dp', 'expert'), axis=0, tiled=True)]
    unnamed x14 -> x7, waiting for transfers between devices: 99.4 us -> 1.44 us
    dot_general x58 -> x32, matrix products: 180 us -> 85.4 us  [dot(): lax.dot_general(a, b, (((da,), (db,)), ((), ())), preferred_element_type=...]
    unnamed x2 -> x0, blocking collectives: 83.2 us -> none
  transfers between devices with their start and end apart: 19 -> 45, of which waited for: 15 -> 20; matrix products, arithmetic and copies ran while one was open for 17% -> 29% of each run, Pallas kernels for 0% -> 4%
where the time goes in v1:
time: 658 us; the launch traced here: 650 us
  waiting for transfers between devices  338 us (51%)
  matrix products  85.4 us (13%)
  local copies, waits for them, and re-layouts  63.9 us (10%)
  other arithmetic  62.8 us (10%)
  starting transfers between devices  60.2 us (9%)
  Pallas kernels  23.1 us (4%)
  between operations  16.3 us (2%)
    dot_general x32, matrix products, dot(): lax.dot_general(a, b, (((da,), (db,)), ((), ())), preferred_element_type=...  85.4 us
    ppermute x16, waiting for transfers between devices, gather_bits(): other = lax.ppermute(x, axis, SWAP)  74.7 us
    ppermute x1, waiting for transfers between devices, on_device(): lax.ppermute(lax.dynamic_index_in_dim(tokens, 1 - mine, 0, keepdims=False...  70.6 us
    reduce_scatter x1, waiting for transfers between devices, on_device(): lax.psum_scatter(dense.astype(bf16), ex_axes, scatter_dimension=0, tiled=...  66.6 us
    all_to_all x1, waiting for transfers between devices, on_device(): lax.all_to_all(payload, ex_axes, 0, 0, tiled=True)  56 us
    ppermute x12, waiting for transfers between devices, scatter_bits(): other = lax.ppermute(send.astype(bf16), axis, SWAP)  39.4 us
    another operation x29, other arithmetic, gather_bits(): jnp.stack([jnp.where(first, x, other), jnp.where(first, other, x)], place)  25 us
    unnamed x220, local copies, waits for them, and re-layouts  20.1 us
  transfers between devices with their start and end apart: 45, of which 20 were waited for; matrix products, arithmetic and copies ran while one was open for 29% of the time, Pallas kernels for 4%

profile of v1, /device:TPU:0, one launch (start us, length us, event | category | flops | bytes accessed | tf_op | source)
XLA Modules:
  0.0 650.0 jit_solution(12200398916838939435)
XLA Ops:
  20.0 70.6 %collective-permute-done = bf16[64,1536]{1,0:T(8,128)(2,1)S(1)} collective-permute-done((bf16[64,1536]{1,0:T(8,128)(2,1)S(1)}, bf16[64,1536]{1,0:T(8,128)(2,1)S(1)}, u32[]{:S(2)}, u32[]{:S(2)}) %collective-permute-start) | collective-permute-done | bytes 196640 | tf_op jit(solution)/shard_map/ppermute | solution.py:340
  101.0 6.1 collective-permute-done.1
  112.5 7.7 %collective-permute-done.4 = bf16[2,64,1536]{2,1,0:T(8,128)(2,1)S(1)} collective-permute-done((bf16[2,64,1536]{2,1,0:T(8,128)(2,1)S(1)}, bf16[2,64,1536]{2,1,0:T(8,128)(2,1)S(1)}, u32[]{:S(2)}, u32[]{:S(2)}) %collective-permute-start.4) | collective-permute-done | bytes 393248 | tf_op jit(solution)/shard_map/ppermute | solution.py:39
  132.4 13.4 %collective-permute-done.3 = bf16[2,2,64,1536]{3,2,1,0:T(8,128)(2,1)} collective-permute-done((bf16[2,2,64,1536]{3,2,1,0:T(8,128)(2,1)}, bf16[2,2,64,1536]{3,2,1,0:T(8,128)(2,1)}, u32[]{:S(2)}, u32[]{:S(2)}) %collective-permute-start.3) | collective-permute-done | bytes 786464 | tf_op jit(solution)/shard_map/ppermute | solution.py:39
  156.0 5.7 shard_map.188
  162.5 6.7 %all-to-all-start.1 = ((bf16[16,64,256]{2,1,0:T(8,128)(2,1)}), bf16[16,64,256]{2,1,0:T(8,128)(2,1)}, u32[]{:S(2)}, u32[]{:S(2)}) async-start(bf16[16,64,256]{2,1,0:T(8,128)(2,1)} %bitcast.41), calls=%async_computation.1 | async-start | bytes 1048576 | tf_op jit(solution)/shard_map/all_to_all | solution.py:375
  176.2 11.2 %all-to-all-done.1 = bf16[16,64,256]{2,1,0:T(8,128)(2,1)} async-done(((bf16[16,64,256]{2,1,0:T(8,128)(2,1)}), bf16[16,64,256]{2,1,0:T(8,128)(2,1)}, u32[]{:S(2)}, u32[]{:S(2)}) %all-to-all-start.1) | async-done | bytes 524320 | tf_op jit(solution)/shard_map/all_to_all | solution.py:375
  200.0 12.7 %collective-permute-done.7 = bf16[64,1664]{1,0:T(8,128)(2,1)S(1)} collective-permute-done((bf16[64,1664]{1,0:T(8,128)(2,1)S(1)}, bf16[64,1664]{1,0:T(8,128)(2,1)S(1)}, u32[]{:S(2)}, u32[]{:S(2)}) %collective-permute-start.7) | collective-permute-done | bytes 213024 | tf_op jit(solution)/shard_map/ppermute | solution.py:39
  214.5 9.5 %collective-permute-done.16 = bf16[64,1664]{1,0:T(8,128)(2,1)S(1)} collective-permute-done((bf16[64,1664]{1,0:T(8,128)(2,1)S(1)}, bf16[64,1664]{1,0:T(8,128)(2,1)S(1)}, u32[]{:S(2)}, u32[]{:S(2)}) %collective-permute-start.16) | collective-permute-done | bytes 213024 | tf_op jit(solution)/shard_map/ppermute | solution.py:39
  228.4 8.3 %collective-permute-done.17 = bf16[2,64,1664]{2,1,0:T(8,128)(2,1)S(1)} collective-permute-done((bf16[2,64,1664]{2,1,0:T(8,128)(2,1)S(1)}, bf16[2,64,1664]{2,1,0:T(8,128)(2,1)S(1)}, u32[]{:S(2)}, u32[]{:S(2)}) %collective-permute-start.17) | collective-permute-done | bytes 426016 | tf_op jit(solution)/shard_map/ppermute | solution.py:39
  239.5 14.8 %collective-permute-done.9 = bf16[2,2,64,1664]{3,2,0,1:T(8,128)(2,1)S(1)} collective-permute-done((bf16[2,2,64,1664]{3,2,0,1:T(8,128)(2,1)S(1)}, bf16[2,2,64,1664]{3,2,0,1:T(8,128)(2,1)S(1)}, u32[]{:S(2)}, u32[]{:S(2)}) %collective-permute-start.9) | collective-permute-done | bytes 852000 | tf_op jit(solution)/shard_map/ppermute | solution.py:39
  266.3 5.6 multiply_convert_fusion.3
  282.2 5.6 fusion.64
  291.0 5.6 multiply_convert_fusion.7
  360.8 12.3 %collective-permute-done.19 = bf16[2,2,64,1664]{3,2,0,1:T(8,128)(2,1)S(1)} collective-permute-done((bf16[2,2,64,1664]{3,2,0,1:T(8,128)(2,1)S(1)}, bf16[2,2,64,1664]{3,2,0,1:T(8,128)(2,1)S(1)}, u32[]{:S(2)}, u32[]{:S(2)}) %collective-permute-start.19) | collective-permute-done | bytes 852000 | tf_op jit(solution)/shard_map/ppermute | solution.py:54
  373.7 7.0 %collective-permute-done.23 = bf16[2,64,1664]{2,1,0:T(8,128)(2,1)S(1)} collective-permute-done((bf16[2,64,1664]{2,1,0:T(8,128)(2,1)S(1)}, bf16[2,64,1664]{2,1,0:T(8,128)(2,1)S(1)}, u32[]{:S(2)}, u32[]{:S(2)}) %collective-permute-start.23) | collective-permute-done | bytes 426016 | tf_op jit(solution)/shard_map/ppermute | solution.py:54
  384.0 15.4 %collective-permute-done.24 = bf16[64,1664]{1,0:T(8,128)(2,1)S(1)} collective-permute-done((bf16[64,1664]{1,0:T(8,128)(2,1)S(1)}, bf16[64,1664]{1,0:T(8,128)(2,1)S(1)}, u32[]{:S(2)}, u32[]{:S(2)}) %collective-permute-start.24) | collective-permute-done | bytes 213024 | tf_op jit(solution)/shard_map/ppermute | solution.py:54
  447.2 56.0 %all-to-all-done.2 = bf16[16,64,256]{2,1,0:T(8,128)(2,1)S(1)} async-done(((bf16[16,64,256]{2,1,0:T(8,128)(2,1)}), bf16[16,64,256]{2,1,0:T(8,128)(2,1)S(1)}, u32[]{:S(2)}, u32[]{:S(2)}) %all-to-all-start.2) | async-done | bytes 524320 | tf_op jit(solution)/shard_map/all_to_all | solution.py:477
  503.2 12.8 %shard_map.189 = bf16[1024,384]{1,0:T(8,128)(2,1)} custom-call(bf16[3,1024,256]{2,1,0:T(8,128)(2,1)} %copy-done.4, bf16[1024,256]{1,0:T(8,128)(2,1)S(1)} %copy-done.7, bf16[3,1024,256]{2,1,0:T(8,128)(2,1)} %copy-done.5, bf16[1024,256]{1,0:T(8,128)(2,1)S(1)} %bitcast.369, f32[1024,128]{1,0:T(8,128)S(1)} %copy-done.9, s32[1024,1]{1,0:T(8,128)} %copy-done.2, ...), custom_call_target="tpu_custom_call" | custom-call | flops 4026531840 | bytes 8388608 | tf_op jit(solution)/shard_map/pallas_call | solution.py:226
  533.5 12.5 %all-to-all-done.3 = bf16[16,64,384]{2,1,0:T(8,128)(2,1)} async-done(((bf16[16,64,384]{2,1,0:T(8,128)(2,1)}), bf16[16,64,384]{2,1,0:T(8,128)(2,1)}, u32[]{:S(2)}, u32[]{:S(2)}) %all-to-all-start.3) | async-done | bytes 786464 | tf_op jit(solution)/shard_map/all_to_all | solution.py:490
  546.0 6.4 all-to-all-start.4
  555.4 6.1 multiply_reduce_fusion.1
  562.7 5.6 all-to-all-done.4
  571.6 66.6 %reduce-scatter.8.cloned.1.call-done = bf16[48,1664]{1,0:T(8,128)(2,1)} async-done(((bf16[768,1664]{1,0:T(8,128)(2,1)}), bf16[48,1664]{1,0:T(8,128)(2,1)}) %reduce-scatter.8.cloned.1.call-update) | async-done | bytes 159760 | tf_op jit(solution)/shard_map/reduce_scatter | solution.py:486
  (501 shorter events, 249.5 us)
Async XLA Ops:
  7.2 182.1 %all-gather.7.cloned.1.call-start = ((), (), s32[]{:S(2)}) async-start(), calls=%async_computation.8 | async-start | bytes 4866048 | tf_op jit(solution)/shard_map/all_gather | solution.py:359
  7.9 258.4 %all-gather.13.cloned.1.call-start = ((), (), s32[]{:S(2)}) async-start(), calls=%async_computation.14 | async-start | bytes 1769472 | tf_op jit(solution)/shard_map/all_gather | solution.py:361
  9.8 118.8 %collective-permute-start.10 = (bf16[768,1024]{1,0:T(8,128)(2,1)}, bf16[768,1024]{1,0:T(8,128)(2,1)}, u32[]{:S(2)}, u32[]{:S(2)}) collective-permute-start(bf16[768,1024]{1,0:T(8,128)(2,1)} %bitcast.434), channel_id=1, source_target_pairs={{0,16},{16,0},{1,17},{17,1},{2,18},{18,2},{3,19},{19,3},{4,20},{20... | collective-permute-start | bytes 4718600 | tf_op jit(solution)/shard_map/ppermute | solution.py:39
  10.3 118.3 %collective-permute-start.12 = (bf16[768,1024]{1,0:T(8,128)(2,1)}, bf16[768,1024]{1,0:T(8,128)(2,1)}, u32[]{:S(2)}, u32[]{:S(2)}) collective-permute-start(bf16[768,1024]{1,0:T(8,128)(2,1)} %bitcast.435), channel_id=1, source_target_pairs={{0,4},{4,0},{1,5},{5,1},{2,6},{6,2},{3,7},{7,3},{8,12},{12,8},{9,1... | collective-permute-start | bytes 4718600 | tf_op jit(solution)/shard_map/ppermute | solution.py:367
  13.0 95.3 %collective-permute-start.11 = (bf16[256,1536]{1,0:T(8,128)(2,1)}, bf16[256,1536]{1,0:T(8,128)(2,1)}, u32[]{:S(2)}, u32[]{:S(2)}) collective-permute-start(bf16[256,1536]{1,0:T(8,128)(2,1)} %bitcast.445), channel_id=1, source_target_pairs={{0,16},{16,0},{1,17},{17,1},{2,18},{18,2},{3,19},{19,3},{4,20},{20... | collective-permute-start | bytes 2359304 | tf_op jit(solution)/shard_map/ppermute | solution.py:39
  13.1 96.7 %collective-permute-start.14 = (bf16[256,1536]{1,0:T(8,128)(2,1)}, bf16[256,1536]{1,0:T(8,128)(2,1)}, u32[]{:S(2)}, u32[]{:S(2)}) collective-permute-start(bf16[256,1536]{1,0:T(8,128)(2,1)} %bitcast.446), channel_id=1, source_target_pairs={{0,4},{4,0},{1,5},{5,1},{2,6},{6,2},{3,7},{7,3},{8,12},{12,8},{9,1... | collective-permute-start | bytes 2359304 | tf_op jit(solution)/shard_map/ppermute | solution.py:368
  14.4 76.3 %collective-permute-start = (bf16[64,1536]{1,0:T(8,128)(2,1)S(1)}, bf16[64,1536]{1,0:T(8,128)(2,1)S(1)}, u32[]{:S(2)}, u32[]{:S(2)}) collective-permute-start(bf16[64,1536]{1,0:T(8,128)(2,1)S(1)} %dynamic-slice_bitcast_fusion.4), channel_id=1, source_target_pairs={{0,8},{8,0},{1,9},{9,1},{2,10},{10,2},{3,11},{11,3},{4,12},{12,4},... | collective-permute-start | bytes 589832 | tf_op jit(solution)/shard_map/ppermute | solution.py:340
  95.4 30.5 %all-to-all-start = ((bf16[16,64,384]{2,1,0:T(8,128)(2,1)}), bf16[16,64,384]{2,1,0:T(8,128)(2,1)S(1)}, u32[]{:S(2)}, u32[]{:S(2)}) async-start(bf16[16,64,384]{2,1,0:T(8,128)(2,1)} %bitcast.36), calls=%async_computation | async-start | bytes 1572864 | tf_op jit(solution)/shard_map/all_to_all | solution.py:322
  100.0 190.9 %all-gather.11.cloned.1.call-start = ((), (), s32[]{:S(2)}) async-start(), calls=%async_computation.13 | async-start | bytes 1769472 | tf_op jit(solution)/shard_map/all_gather | solution.py:361
  109.8 63.6 %collective-permute-start.15 = (bf16[256,1536]{1,0:T(8,128)(2,1)}, bf16[256,1536]{1,0:T(8,128)(2,1)}, u32[]{:S(2)}, u32[]{:S(2)}) collective-permute-start(bf16[256,1536]{1,0:T(8,128)(2,1)} %collective-permute-done.14), channel_id=1, source_target_pairs={{0,16},{16,0},{1,17},{17,1},{2,18},{18,2},{3,19},{19,3},{4,20},{20... | collective-permute-start | bytes 2359304 | tf_op jit(solution)/shard_map/ppermute | solution.py:39
  128.7 69.2 %collective-permute-start.13 = (bf16[768,1024]{1,0:T(8,128)(2,1)}, bf16[768,1024]{1,0:T(8,128)(2,1)}, u32[]{:S(2)}, u32[]{:S(2)}) collective-permute-start(bf16[768,1024]{1,0:T(8,128)(2,1)} %collective-permute-done.12), channel_id=1, source_target_pairs={{0,16},{16,0},{1,17},{17,1},{2,18},{18,2},{3,19},{19,3},{4,20},{20... | collective-permute-start | bytes 4718600 | tf_op jit(solution)/shard_map/ppermute | solution.py:39
  169.2 239.0 %reduce-scatter.6.cloned.1.call-start = ((), (), s32[]{:S(2)}) async-start(), calls=%async_computation.10 | async-start | bytes 1769472 | tf_op jit(solution)/shard_map/reduce_scatter | solution.py:435
  282.0 126.2 %reduce-scatter.4.cloned.1.call-start = ((), (), s32[]{:S(2)}) async-start(), calls=%async_computation.9 | async-start | bytes 1769472 | tf_op jit(solution)/shard_map/reduce_scatter | solution.py:435
  305.5 249.8 %all-gather.9.cloned.1.call-start = ((), (), s32[]{:S(2)}) async-start(), calls=%async_computation.11 | async-start | bytes 8110080 | tf_op jit(solution)/shard_map/all_gather | solution.py:364
  328.5 28.5 %collective-permute-start.22 = (bf16[2,2,64,1664]{3,2,0,1:T(8,128)(2,1)}, bf16[2,2,64,1664]{3,2,0,1:T(8,128)(2,1)}, u32[]{:S(2)}, u32[]{:S(2)}) collective-permute-start(bf16[2,2,64,1664]{3,2,0,1:T(8,128)(2,1)} %bitcast.357), channel_id=1, source_target_pairs={{0,1},{1,0},{2,3},{3,2},{4,5},{5,4},{6,7},{7,6},{8,9},{9,8},{10,11... | collective-permute-start | bytes 2555912 | tf_op jit(solution)/shard_map/ppermute | solution.py:54
  344.4 28.7 %collective-permute-start.19 = (bf16[2,2,64,1664]{3,2,0,1:T(8,128)(2,1)S(1)}, bf16[2,2,64,1664]{3,2,0,1:T(8,128)(2,1)S(1)}, u32[]{:S(2)}, u32[]{:S(2)}) collective-permute-start(bf16[2,2,64,1664]{3,2,0,1:T(8,128)(2,1)S(1)} %bitcast.442), channel_id=1, source_target_pairs={{0,2},{2,0},{1,3},{3,1},{4,6},{6,4},{5,7},{7,5},{8,10},{10,8},{9,1... | collective-permute-start | bytes 2555912 | tf_op jit(solution)/shard_map/ppermute | solution.py:54
  353.2 72.9 %collective-permute-start.28 = (bf16[768,1024]{1,0:T(8,128)(2,1)}, bf16[768,1024]{1,0:T(8,128)(2,1)}, u32[]{:S(2)}, u32[]{:S(2)}) collective-permute-start(bf16[768,1024]{1,0:T(8,128)(2,1)} %fusion.15), channel_id=1, source_target_pairs={{0,16},{16,0},{1,17},{17,1},{2,18},{18,2},{3,19},{19,3},{4,20},{20... | collective-permute-start | bytes 4718600 | tf_op jit(solution)/shard_map/ppermute | solution.py:54
  357.0 171.0 %collective-permute-start.27 = (bf16[768,1024]{1,0:T(8,128)(2,1)}, bf16[768,1024]{1,0:T(8,128)(2,1)}, u32[]{:S(2)}, u32[]{:S(2)}) collective-permute-start(bf16[768,1024]{1,0:T(8,128)(2,1)} %fusion.14), channel_id=1, source_target_pairs={{0,16},{16,0},{1,17},{17,1},{2,18},{18,2},{3,19},{19,3},{4,20},{20... | collective-permute-start | bytes 4718600 | tf_op jit(solution)/shard_map/ppermute | solution.py:54
  425.9 99.3 %collective-permute-start.30 = (bf16[256,1536]{1,0:T(8,128)(2,1)}, bf16[256,1536]{1,0:T(8,128)(2,1)}, u32[]{:S(2)}, u32[]{:S(2)}) collective-permute-start(bf16[256,1536]{1,0:T(8,128)(2,1)} %fusion.71), channel_id=1, source_target_pairs={{0,16},{16,0},{1,17},{17,1},{2,18},{18,2},{3,19},{19,3},{4,20},{20... | collective-permute-start | bytes 2359304 | tf_op jit(solution)/shard_map/ppermute | solution.py:54
  431.7 96.3 %collective-permute-start.29 = (bf16[768,1024]{1,0:T(8,128)(2,1)}, bf16[768,1024]{1,0:T(8,128)(2,1)}, u32[]{:S(2)}, u32[]{:S(2)}) collective-permute-start(bf16[768,1024]{1,0:T(8,128)(2,1)} %fusion.1), channel_id=1, source_target_pairs={{0,4},{4,0},{1,5},{5,1},{2,6},{6,2},{3,7},{7,3},{8,12},{12,8},{9,1... | collective-permute-start | bytes 4718600 | tf_op jit(solution)/shard_map/ppermute | solution.py:451
  434.0 69.2 %all-to-all-start.2 = ((bf16[16,64,256]{2,1,0:T(8,128)(2,1)}), bf16[16,64,256]{2,1,0:T(8,128)(2,1)S(1)}, u32[]{:S(2)}, u32[]{:S(2)}) async-start(bf16[16,64,256]{2,1,0:T(8,128)(2,1)} %bitcast.101), calls=%async_computation.4 | async-start | bytes 1048576 | tf_op jit(solution)/shard_map/all_to_all | solution.py:477
  437.9 200.4 %reduce-scatter.8.cloned.1.call-start = ((), (), s32[]{:S(2)}) async-start(), calls=%async_computation.12 | async-start | bytes 2715648 | tf_op jit(solution)/shard_map/reduce_scatter | solution.py:486
  445.3 79.9 %collective-permute-start.32 = (bf16[256,1536]{1,0:T(8,128)(2,1)}, bf16[256,1536]{1,0:T(8,128)(2,1)}, u32[]{:S(2)}, u32[]{:S(2)}) collective-permute-start(bf16[256,1536]{1,0:T(8,128)(2,1)} %fusion.16), channel_id=1, source_target_pairs={{0,4},{4,0},{1,5},{5,1},{2,6},{6,2},{3,7},{7,3},{8,12},{12,8},{9,1... | collective-permute-start | bytes 2359304 | tf_op jit(solution)/shard_map/ppermute | solution.py:451
  516.1 29.9 %all-to-all-start.3 = ((bf16[16,64,384]{2,1,0:T(8,128)(2,1)}), bf16[16,64,384]{2,1,0:T(8,128)(2,1)}, u32[]{:S(2)}, u32[]{:S(2)}) async-start(bf16[16,64,384]{2,1,0:T(8,128)(2,1)} %bitcast.443), calls=%async_computation.5 | async-start | bytes 1572864 | tf_op jit(solution)/shard_map/all_to_all | solution.py:490
  (124 other events, 1566.6 us)
Sparse Core Ops, SparseCore 0:
  10.9 75.6 all-gather.6
  88.8 58.4 all-gather.12
  149.5 63.0 all-gather.10
  282.1 51.0 reduce-scatter.5
  336.8 60.4 reduce-scatter.3
  400.6 90.3 all-gather.8
  496.0 142.2 reduce-scatter.7
